TPU v7x, 256 devices: a whole 4x4x8 slice. The times are simulated.
256 devices in a mesh: tm: 32 (over x, y, core), space: 8 (over z).
Axes of the slice: x: 4, y: 4, z: 8, core: 2. Of those that a mesh axis runs over, the one named last changes fastest.
Arguments:
- sep_block: float32 [32, 1536, 1536], P('tm', 'space'), may hold values from -1 to 10, as said below
- own_couple: bfloat16 [32, 1536, 1536], P('tm', 'space'), may hold values from -0.1875 to 0.1875
- prev_couple: bfloat16 [32, 1536, 1536], P('tm', 'space'), may hold values from -0.1875 to 0.1875
- inner_diag: float32 [32, 1536], P('tm'), may hold values from 0.5 to 4
Outputs:
- reduced_blocks: float32 [32, 1536, 1536], P('tm', 'space')
- left_links: bfloat16 [32, 1536, 1536], P('tm', 'space')
Inputs may be any that keep to these rules, and one draw needn't show every extreme that they name: sep_block is symmetric in its last two dimensions; its diagonal entries lie between 3.5 and 10.
All inputs are finite; a program needn't handle non-finite values.
Results may differ from a plain program's by a relative error of at most 0.0083.
Values may be sent and summed in bfloat16 or wider, within the bound.
A program may use at most 64 MiB of HBM per device.

v0:
```python
import jax
import jax.numpy as jnp
from jax import lax
from jax.sharding import PartitionSpec as P


def passed_along(block, axis, distance):
    devices = range(lax.axis_size(axis))
    route = [(i - distance, i) for i in devices if i - distance in devices]
    return lax.ppermute(block, axis, route)


def scaled_by(matrix, factors):
    return (matrix.astype(jnp.float32) * factors.astype(jnp.float32)[None, :]).astype(jnp.bfloat16)


def outer_form(left_side, right_side):
    return jnp.einsum("ik,jk->ij", left_side, right_side, preferred_element_type=jnp.float32)


def reduce_level(schur, link, distance, partition, row_start):
    row_count = schur.shape[0]
    diag_block = lax.dynamic_slice_in_dim(schur, row_start, row_count, 1)
    scale_local = (1.0 / jnp.maximum(jnp.diagonal(diag_block), 1.0)).astype(jnp.bfloat16)
    scale_full = lax.all_gather(scale_local, "space", axis=0, tiled=True)
    own_full = lax.all_gather(link, "space", axis=0, tiled=True)
    next_full, next_scale = passed_along((own_full, scale_full), "tm", -distance)
    flipped = lax.dynamic_slice_in_dim(next_full, row_start, row_count, 1).T
    flipped_scaled = scaled_by(flipped, scale_full)
    right_form = jnp.dot(flipped_scaled, next_full, preferred_element_type=jnp.float32)
    own_scaled = scaled_by(link, scale_full)
    fill_link = (-jnp.dot(own_scaled, next_full, preferred_element_type=jnp.float32)).astype(
        jnp.bfloat16
    )
    right_recv, fill_recv = (
        passed_along(right_form.astype(jnp.bfloat16), "tm", distance).astype(right_form.dtype),
        passed_along(fill_link.astype(jnp.float32).astype(jnp.bfloat16), "tm", distance).astype(
            jnp.float32
        ),
    )
    next_local = lax.dynamic_slice_in_dim(next_full, row_start, row_count, 0)
    next_scaled = scaled_by(next_local, next_scale)
    left_form = outer_form(next_scaled, next_full)
    new_schur = schur - left_form - right_recv
    receiver = partition % (2 * distance) == 2 * distance - 1
    return (
        jnp.where(receiver, new_schur, schur),
        jnp.where(receiver, fill_recv.astype(jnp.bfloat16), link),
    )


def on_device(sep_block, own_couple, prev_couple, inner_diag):
    separator = sep_block[0]
    own_rows = own_couple[0]
    prev_rows = prev_couple[0]
    reciprocal = 1.0 / inner_diag[0]
    row_count = separator.shape[0]
    row_start = lax.axis_index("space") * row_count
    partition = lax.axis_index("tm")
    own_scaled = scaled_by(own_rows, reciprocal)
    prev_scaled = scaled_by(prev_rows, reciprocal)
    couple_pair = jnp.stack([own_rows, prev_rows])
    piece_rows = lax.all_gather(couple_pair, "space", axis=1, tiled=True)
    local_forms = jnp.stack(
        [
            outer_form(own_scaled, piece_rows[0]),
            outer_form(prev_scaled, piece_rows[1]),
            outer_form(prev_scaled, piece_rows[0]),
        ]
    )
    incoming = passed_along(local_forms[1], "tm", -1)
    schur = separator - local_forms[0] - incoming
    link = (-local_forms[2]).astype(jnp.bfloat16)
    link = jnp.where(partition == 0, jnp.zeros_like(link), link)
    for distance in (1, 2):
        schur, link = reduce_level(schur, link, distance, partition, row_start)
    return (schur[None], link[None])


def solution(mesh):
    placed = (P("tm", "space", None), P("tm", "space", None), P("tm", "space", None), P("tm", None))
    return jax.shard_map(
        on_device,
        mesh=mesh,
        in_specs=placed,
        out_specs=(P("tm", "space", None), P("tm", "space", None)),
        check_vma=False,
    )
```

profile of v0, /device:TPU:6, one launch (start us, length us, event | category | flops | bytes accessed | tf_op | source)
XLA Modules:
  0.0 520.2 jit_solution(10280945665940516997)
XLA Ops:
  7.2 0.0 all-gather.4.cloned.1.call-start
  7.2 2.4 pad_maximum_fusion
  9.6 0.0 copy-start.5
  9.6 0.0 copy-start.4
  9.6 0.0 all-gather.4.cloned.1.call-update
  9.6 0.0 all-gather.6.cloned.1.call-start
  9.7 0.6 copy-done.5
  10.3 107.0 %all-gather.4.cloned.1.call-done = bf16[2,1536,1536]{2,1,0:T(8,128)(2,1)} async-done(((bf16[2,192,1536]{2,1,0:T(8,128)(2,1)}), bf16[2,1536,1536]{2,1,0:T(8,128)(2,1)}) %all-gather.4.cloned.1.call-update) | async-done | bytes 9437200 | tf_op jit(solution)/shard_map/all_gather | solution.py:63
  117.3 0.0 copy-done.4
  117.3 4.8 fusion.14
  122.1 0.0 all-gather.6.cloned.1.call-update
  122.1 0.0 copy-start.6
  122.2 0.0 copy-start.1
  122.2 0.0 copy-start.3
  122.2 0.0 all-gather.8.cloned.1.call-start
  122.2 58.4 %all-gather.6.cloned.1.call-done = bf16[1536,1536]{1,0:T(8,128)(2,1)} async-done(((bf16[192,1536]{1,0:T(8,128)(2,1)}), bf16[1536,1536]{1,0:T(8,128)(2,1)}) %all-gather.6.cloned.1.call-update) | async-done | bytes 4718608 | tf_op jit(solution)/shard_map/all_gather | solution.py:26
  180.6 4.4 collective-permute-start.1
  185.0 5.0 fusion
  190.1 2.6 collective-permute-start
  192.6 0.0 copy-done.6
  192.7 0.6 dynamic-slice
  193.8 55.8 %collective-permute-done = f32[192,1536]{1,0:T(8,128)} collective-permute-done((f32[192,1536]{1,0:T(8,128)}, f32[192,1536]{1,0:T(8,128)}, u32[]{:S(2)}, u32[]{:S(2)}) %collective-permute-start) | collective-permute-done | bytes 1179680 | tf_op jit(solution)/shard_map/ppermute | solution.py:10
  249.6 0.0 copy-done.1
  249.6 0.0 copy-done.3
  249.6 4.4 fusion.4
  254.0 0.0 copy-start.2
  254.0 0.1 constant_dynamic-slice_fusion.1
  254.2 1.9 gather_fusion
  256.1 0.2 dynamic-update-slice
  256.4 15.5 %all-reduce = bf16[1536]{0:T(1024)(128)(2,1)S(1)} all-reduce(bf16[1536]{0:T(1024)(128)(2,1)S(1)} %dynamic-update-slice), channel_id=1, replica_groups=mesh['tm'=32,'space'=8] {'space'}, use_global_device_ids=true, to_apply=%add | all-reduce | flops 1536 | bytes 6144
  271.9 0.0 collective-permute-done.1
  271.9 0.0 copy-done.2
  271.9 3.4 fusion.12
  275.3 1.9 collective-permute-start.4
  277.3 11.4 %collective-permute-done.4 = bf16[192,1536]{1,0:T(8,128)(2,1)S(1)} collective-permute-done((bf16[192,1536]{1,0:T(8,128)(2,1)S(1)}, bf16[192,1536]{1,0:T(8,128)(2,1)S(1)}, u32[]{:S(2)}, u32[]{:S(2)}) %collective-permute-start.4) | collective-permute-done | bytes 589856 | tf_op jit(solution)/shard_map/ppermute | solution.py:10
  288.6 0.9 broadcast_select_fusion
  289.5 0.0 all-gather.8.cloned.1.call-update
  289.5 57.0 %all-gather.8.cloned.1.call-done = bf16[1536,1536]{1,0:T(8,128)(2,1)} async-done(((bf16[192,1536]{1,0:T(8,128)(2,1)}), bf16[1536,1536]{1,0:T(8,128)(2,1)}) %all-gather.8.cloned.1.call-update) | async-done | bytes 4718608 | tf_op jit(solution)/shard_map/all_gather | solution.py:26
  346.6 4.9 collective-permute-start.5
  351.5 4.0 convolution_convert_fusion.1
  355.4 1.9 collective-permute-start.3
  357.4 5.8 %collective-permute-start.2 = (bf16[1536]{0:T(1024)(128)(2,1)S(1)}, bf16[1536]{0:T(1024)(128)(2,1)S(1)}, u32[]{:S(2)}, u32[]{:S(2)}) collective-permute-start(bf16[1536]{0:T(1024)(128)(2,1)S(1)} %all-reduce), channel_id=1, source_target_pairs={{8,0},{16,8},{24,16},{32,24},{40,32},{48,40},{56,48},{64,56},{72,6... | collective-permute-start | bytes 9224 | tf_op jit(solution)/shard_map/ppermute | solution.py:10
  363.1 89.7 %collective-permute-done.2 = bf16[1536]{0:T(1024)(128)(2,1)S(1)} collective-permute-done((bf16[1536]{0:T(1024)(128)(2,1)S(1)}, bf16[1536]{0:T(1024)(128)(2,1)S(1)}, u32[]{:S(2)}, u32[]{:S(2)}) %collective-permute-start.2) | collective-permute-done | bytes 3104 | tf_op jit(solution)/shard_map/ppermute | solution.py:10
  452.8 0.0 collective-permute-done.3
  452.9 4.2 fusion.9
  457.1 0.0 copy-start
  457.1 0.1 constant_dynamic-slice_fusion
  457.2 1.9 gather_fusion.1
  459.2 0.2 dynamic-update-slice.1
  459.4 15.5 %all-reduce.1 = bf16[1536]{0:T(1024)(128)(2,1)S(1)} all-reduce(bf16[1536]{0:T(1024)(128)(2,1)S(1)} %dynamic-update-slice.1), channel_id=1, replica_groups=mesh['tm'=32,'space'=8] {'space'}, use_global_device_ids=true, to_apply=%add.1 | all-reduce | flops 1536 | bytes 6144
  474.9 0.0 collective-permute-done.5
  474.9 0.0 copy-done
  475.0 4.3 fusion.13
  479.2 1.9 collective-permute-start.8
  481.1 3.9 convolution_convert_fusion
  485.1 2.4 collective-permute-start.7
  487.5 5.6 %collective-permute-start.6 = (bf16[1536]{0:T(1024)(128)(2,1)S(1)}, bf16[1536]{0:T(1024)(128)(2,1)S(1)}, u32[]{:S(2)}, u32[]{:S(2)}) collective-permute-start(bf16[1536]{0:T(1024)(128)(2,1)S(1)} %all-reduce.1), channel_id=1, source_target_pairs={{16,0},{24,8},{32,16},{40,24},{48,32},{56,40},{64,48},{72,56},{80,... | collective-permute-start | bytes 9224 | tf_op jit(solution)/shard_map/ppermute | solution.py:10
  493.1 1.3 collective-permute-done.6
  494.4 5.3 %collective-permute-done.8 = bf16[192,1536]{1,0:T(8,128)(2,1)S(1)} collective-permute-done((bf16[192,1536]{1,0:T(8,128)(2,1)}, bf16[192,1536]{1,0:T(8,128)(2,1)S(1)}, u32[]{:S(2)}, u32[]{:S(2)}) %collective-permute-start.8) | collective-permute-done | bytes 589856 | tf_op jit(solution)/shard_map/ppermute | solution.py:10
  499.7 0.9 select_bitcast_fusion
  500.6 7.8 %collective-permute-done.7 = bf16[192,1536]{1,0:T(8,128)(2,1)S(1)} collective-permute-done((bf16[192,1536]{1,0:T(8,128)(2,1)S(1)}, bf16[192,1536]{1,0:T(8,128)(2,1)S(1)}, u32[]{:S(2)}, u32[]{:S(2)}) %collective-permute-start.7) | collective-permute-done | bytes 589856 | tf_op jit(solution)/shard_map/ppermute | solution.py:10
  508.4 5.2 %fusion.7 = f32[1,192,1536]{2,1,0:T(8,128)} fusion(f32[192,1536]{1,0:T(8,128)S(1)} %fusion.9, bf16[1536,1536]{1,0:T(8,128)(2,1)} %collective-permute-done.5, bf16[192,1536]{1,0:T(8,128)(2,1)S(1)} %collective-permute-done.7, f32[1536]{0:T(1024)S(1)} %convert_element_type.132, s32[]{:T(128)S(6)} %select_n.61, pred[]{:T(512)S(6)} %eq.12), kind=kOutput, calls=%fused_computation.14 | convolution fusion | flops 908034048 | bytes 8263685 | tf_op jit(solution)/shard_map/ik,jk->ij/dot_general | solution.py:18
  (10 shorter events, 0.1 us)
Async XLA Ops:
  7.2 110.1 %all-gather.4.cloned.1.call-start = ((), (), s32[]{:S(2)}) async-start(), calls=%async_computation | async-start | bytes 10616832 | tf_op jit(solution)/shard_map/all_gather | solution.py:63
  9.6 0.7 copy-start.5
  9.6 107.7 %copy-start.4 = (bf16[1,192,1536]{2,1,0:T(8,128)(2,1)S(1)}, bf16[1,192,1536]{2,1,0:T(8,128)(2,1)}, u32[]{:S(2)}) copy-start(bf16[1,192,1536]{2,1,0:T(8,128)(2,1)} %param.6) | copy-start | bytes 1769476
  9.6 171.0 %all-gather.6.cloned.1.call-start = ((), (), s32[]{:S(2)}) async-start(), calls=%async_computation.1 | async-start | bytes 5308416 | tf_op jit(solution)/shard_map/all_gather | solution.py:26
  122.1 70.5 %copy-start.6 = (u32[256]{0:T(256)S(1)}, u32[256]{0:T(256)}, u32[]{:S(2)}) copy-start(u32[256]{0:T(256)} %constant.83) | copy-start | bytes 3076
  122.2 127.4 %copy-start.1 = (bf16[1,192,1536]{2,1,0:T(8,128)(2,1)S(1)}, bf16[1,192,1536]{2,1,0:T(8,128)(2,1)}, u32[]{:S(2)}) copy-start(bf16[1,192,1536]{2,1,0:T(8,128)(2,1)} %param.5) | copy-start | bytes 1769476
  122.2 127.4 %copy-start.3 = (f32[1,192,1536]{2,1,0:T(8,128)S(1)}, f32[1,192,1536]{2,1,0:T(8,128)}, u32[]{:S(2)}) copy-start(f32[1,192,1536]{2,1,0:T(8,128)} %param.4) | copy-start | bytes 3538948
  122.2 224.4 %all-gather.8.cloned.1.call-start = ((), (), s32[]{:S(2)}) async-start(), calls=%async_computation.2 | async-start | bytes 5308416 | tf_op jit(solution)/shard_map/all_gather | solution.py:26
  180.6 91.2 %collective-permute-start.1 = (bf16[1536,1536]{1,0:T(8,128)(2,1)}, bf16[1536,1536]{1,0:T(8,128)(2,1)}, u32[]{:S(2)}, u32[]{:S(2)}) collective-permute-start(bf16[1536,1536]{1,0:T(8,128)(2,1)} %all-gather.6.cloned.1.call-done), channel_id=1, source_target_pairs={{8,0},{16,8},{24,16},{32,24},{40,32},{48,40},{56,48},{64,56},{72,6... | collective-permute-start | bytes 14155784 | tf_op jit(solution)/shard_map/ppermute | solution.py:10
  190.1 59.5 %collective-permute-start = (f32[192,1536]{1,0:T(8,128)}, f32[192,1536]{1,0:T(8,128)}, u32[]{:S(2)}, u32[]{:S(2)}) collective-permute-start(f32[192,1536]{1,0:T(8,128)} %fusion), channel_id=1, source_target_pairs={{8,0},{16,8},{24,16},{32,24},{40,32},{48,40},{56,48},{64,56},{72,6... | collective-permute-start | bytes 3538952 | tf_op jit(solution)/shard_map/ppermute | solution.py:10
  254.0 17.8 %copy-start.2 = (bf16[192,1536]{1,0:T(8,128)(2,1)S(1)}, bf16[192,1536]{1,0:T(8,128)(2,1)}, u32[]{:S(2)}) copy-start(bf16[192,1536]{1,0:T(8,128)(2,1)} %fusion.14) | copy-start | bytes 1769476
  275.3 13.3 %collective-permute-start.4 = (bf16[192,1536]{1,0:T(8,128)(2,1)S(1)}, bf16[192,1536]{1,0:T(8,128)(2,1)S(1)}, u32[]{:S(2)}, u32[]{:S(2)}) collective-permute-start(bf16[192,1536]{1,0:T(8,128)(2,1)S(1)} %fusion.12), channel_id=1, source_target_pairs={{0,8},{8,16},{16,24},{24,32},{32,40},{40,48},{48,56},{56,64},{64,7... | collective-permute-start | bytes 1769480 | tf_op jit(solution)/shard_map/ppermute | solution.py:10
  346.6 128.4 %collective-permute-start.5 = (bf16[1536,1536]{1,0:T(8,128)(2,1)}, bf16[1536,1536]{1,0:T(8,128)(2,1)}, u32[]{:S(2)}, u32[]{:S(2)}) collective-permute-start(bf16[1536,1536]{1,0:T(8,128)(2,1)} %all-gather.8.cloned.1.call-done), channel_id=1, source_target_pairs={{16,0},{24,8},{32,16},{40,24},{48,32},{56,40},{64,48},{72,56},{80,... | collective-permute-start | bytes 14155784 | tf_op jit(solution)/shard_map/ppermute | solution.py:10
  355.4 97.4 %collective-permute-start.3 = (bf16[192,1536]{1,0:T(8,128)(2,1)S(1)}, bf16[192,1536]{1,0:T(8,128)(2,1)S(1)}, u32[]{:S(2)}, u32[]{:S(2)}) collective-permute-start(bf16[192,1536]{1,0:T(8,128)(2,1)S(1)} %convolution_convert_fusion.1), channel_id=1, source_target_pairs={{0,8},{8,16},{16,24},{24,32},{32,40},{40,48},{48,56},{56,64},{64,7... | collective-permute-start | bytes 1769480 | tf_op jit(solution)/shard_map/ppermute | solution.py:10
  357.4 95.5 %collective-permute-start.2 = (bf16[1536]{0:T(1024)(128)(2,1)S(1)}, bf16[1536]{0:T(1024)(128)(2,1)S(1)}, u32[]{:S(2)}, u32[]{:S(2)}) collective-permute-start(bf16[1536]{0:T(1024)(128)(2,1)S(1)} %all-reduce), channel_id=1, source_target_pairs={{8,0},{16,8},{24,16},{32,24},{40,32},{48,40},{56,48},{64,56},{72,6... | collective-permute-start | bytes 9224 | tf_op jit(solution)/shard_map/ppermute | solution.py:10
  457.1 17.9 %copy-start = (bf16[192,1536]{1,0:T(8,128)(2,1)S(1)}, bf16[192,1536]{1,0:T(8,128)(2,1)}, u32[]{:S(2)}) copy-start(bf16[192,1536]{1,0:T(8,128)(2,1)} %broadcast_select_fusion) | copy-start | bytes 1769476
  479.2 20.5 %collective-permute-start.8 = (bf16[192,1536]{1,0:T(8,128)(2,1)}, bf16[192,1536]{1,0:T(8,128)(2,1)S(1)}, u32[]{:S(2)}, u32[]{:S(2)}) collective-permute-start(bf16[192,1536]{1,0:T(8,128)(2,1)} %fusion.13), channel_id=1, source_target_pairs={{0,16},{8,24},{16,32},{24,40},{32,48},{40,56},{48,64},{56,72},{64,... | collective-permute-start | bytes 1769480 | tf_op jit(solution)/shard_map/ppermute | solution.py:10
  485.1 23.3 %collective-permute-start.7 = (bf16[192,1536]{1,0:T(8,128)(2,1)S(1)}, bf16[192,1536]{1,0:T(8,128)(2,1)S(1)}, u32[]{:S(2)}, u32[]{:S(2)}) collective-permute-start(bf16[192,1536]{1,0:T(8,128)(2,1)S(1)} %convolution_convert_fusion), channel_id=1, source_target_pairs={{0,16},{8,24},{16,32},{24,40},{32,48},{40,56},{48,64},{56,72},{64,... | collective-permute-start | bytes 1769480 | tf_op jit(solution)/shard_map/ppermute | solution.py:10
  487.5 6.9 %collective-permute-start.6 = (bf16[1536]{0:T(1024)(128)(2,1)S(1)}, bf16[1536]{0:T(1024)(128)(2,1)S(1)}, u32[]{:S(2)}, u32[]{:S(2)}) collective-permute-start(bf16[1536]{0:T(1024)(128)(2,1)S(1)} %all-reduce.1), channel_id=1, source_target_pairs={{16,0},{24,8},{32,16},{40,24},{48,32},{56,40},{64,48},{72,56},{80,... | collective-permute-start | bytes 9224 | tf_op jit(solution)/shard_map/ppermute | solution.py:10
Sparse Core Ops, SparseCore 0:
  10.4 106.8 all-gather.3
  122.3 58.3 all-gather.5
  289.7 56.8 all-gather.7
where the time goes:
time: 521 us; the launch traced here: 520 us
  waiting for transfers between devices  394 us (76%)
  matrix products  39.3 us (8%)
  starting transfers between devices  31.4 us (6%)
  blocking collectives  31 us (6%)
  between operations  14.6 us (3%)
  local copies, waits for them, and re-layouts  5.8 us (1%)
    ppermute x9, waiting for transfers between devices, passed_along(): return lax.ppermute(block, axis, route)  171 us
    all_gather x2, waiting for transfers between devices, reduce_level(): own_full = lax.all_gather(link, 'space', axis=0, tiled=True)  115 us
    all_gather x1, waiting for transfers between devices, on_device(): piece_rows = lax.all_gather(couple_pair, 'space', axis=1, tiled=True)  107 us
    ppermute x9, starting transfers between devices, passed_along(): return lax.ppermute(block, axis, route)  31.3 us
    unnamed x2, blocking collectives  31 us
    dot_general x5, matrix products, outer_form(): jnp.einsum('ik,jk->ij', left_side, right_side, preferred_element_type=jnp...  23.8 us
  transfers between devices with their start and end apart: 12, of which 9 were waited for; matrix products, arithmetic and copies ran while one was open for 5% of the time, Pallas kernels for 0%

commit v1 on v0

--- a/solution.py
+++ b/solution.py
@@ -60,7 +60,10 @@
     own_scaled = scaled_by(own_rows, reciprocal)
     prev_scaled = scaled_by(prev_rows, reciprocal)
     couple_pair = jnp.stack([own_rows, prev_rows])
-    piece_rows = lax.all_gather(couple_pair, "space", axis=1, tiled=True)
+    count = lax.axis_size("space")
+    blocks = jnp.stack([couple_pair for _ in range(count)])
+    blocks = lax.all_to_all(blocks, "space", split_axis=0, concat_axis=0)
+    piece_rows = jnp.concatenate(blocks, axis=1)
     local_forms = jnp.stack(
         [
             outer_form(own_scaled, piece_rows[0]),

time: 521 us -> 639 us (1.23)
  waiting for transfers between devices: 394 us -> 493 us
  local copies, waits for them, and re-layouts: 5.8 us -> 18.6 us
  starting transfers between devices: 31.4 us -> 40.2 us
    all_to_all x0 -> x1, waiting for transfers between devices: none -> 209 us  [on_device(): blocks = lax.all_to_all(blocks, 'space', split_axis=0, concat_axis=0)]
    all_gather x1 -> x0, waiting for transfers between devices: 107 us -> none  [on_device(): piece_rows = lax.all_gather(couple_pair, 'space', axis=1, tiled=True)]
    all_to_all x0 -> x1, starting transfers between devices: none -> 8.6 us  [on_device(): blocks = lax.all_to_all(blocks, 'space', split_axis=0, concat_axis=0)]
    slice x0 -> x1, local copies, waits for them, and re-layouts: none -> 6.56 us  [on_device(): piece_rows[0]]
  transfers between devices with their start and end apart: 12 -> 12, of which waited for: 9 -> 9; matrix products, arithmetic and copies ran while one was open for 5% -> 4% of each run, Pallas kernels for 0% -> 0%
where the time goes in v1:
time: 639 us; the launch traced here: 638 us
  waiting for transfers between devices  493 us (77%)
  starting transfers between devices  40.2 us (6%)
  matrix products  37.1 us (6%)
  blocking collectives  31 us (5%)
  local copies, waits for them, and re-layouts  18.6 us (3%)
  between operations  15 us (2%)
    all_to_all x1, waiting for transfers between devices, on_device(): blocks = lax.all_to_all(blocks, 'space', split_axis=0, concat_axis=0)  209 us
    ppermute x9, waiting for transfers between devices, passed_along(): return lax.ppermute(block, axis, route)  171 us
    all_gather x2, waiting for transfers between devices, reduce_level(): own_full = lax.all_gather(link, 'space', axis=0, tiled=True)  113 us
    ppermute x9, starting transfers between devices, passed_along(): return lax.ppermute(block, axis, route)  31.5 us
    unnamed x2, blocking collectives  31 us
    dot_general x5, matrix products, outer_form(): jnp.einsum('ik,jk->ij', left_side, right_side, preferred_element_type=jnp...  21.6 us
  transfers between devices with their start and end apart: 12, of which 9 were waited for; matrix products, arithmetic and copies ran while one was open for 4% of the time, Pallas kernels for 0%

profile of v1, /device:TPU:6, one launch (start us, length us, event | category | flops | bytes accessed | tf_op | source)
XLA Modules:
  0.0 638.2 jit_solution(5741723622056131000)
XLA Ops:
  7.2 1.4 pad_maximum_fusion
  8.5 4.6 stack.5
  13.1 0.0 copy-start.6
  13.1 8.6 %all-to-all-start = ((bf16[8,2,192,1536]{3,2,1,0:T(8,128)(2,1)}), bf16[8,2,192,1536]{3,2,1,0:T(8,128)(2,1)}, u32[]{:S(2)}, u32[]{:S(2)}) async-start(bf16[8,2,192,1536]{3,2,1,0:T(8,128)(2,1)} %stack.5), calls=%async_computation | async-start | bytes 18874368 | tf_op jit(solution)/shard_map/all_to_all | solution.py:65
  21.7 0.0 all-gather.3.cloned.1.call-start
  21.7 0.0 copy-done.6
  21.8 209.1 %all-to-all-done = bf16[8,2,192,1536]{3,2,1,0:T(8,128)(2,1)} async-done(((bf16[8,2,192,1536]{3,2,1,0:T(8,128)(2,1)}), bf16[8,2,192,1536]{3,2,1,0:T(8,128)(2,1)}, u32[]{:S(2)}, u32[]{:S(2)}) %all-to-all-start) | async-done | bytes 9437216 | tf_op jit(solution)/shard_map/all_to_all | solution.py:65
  230.9 0.0 copy-start.5
  230.9 6.6 %fusion.33 = (bf16[1,8,192,1536]{3,2,0,1:T(8,128)(2,1)S(1)}, bf16[1,8,192,1536]{3,2,0,1:T(8,128)(2,1)}) fusion(bf16[2,8,192,1536]{3,2,0,1:T(8,128)(2,1)} %bitcast.2), kind=kLoop, calls=%fused_computation.57 | loop fusion | bytes 18874368 | tf_op jit(solution)/shard_map/slice | solution.py:69
  237.4 2.2 copy-done
  239.7 0.0 copy-done.5
  239.7 2.5 fusion.9
  242.2 0.0 all-gather.3.cloned.1.call-update
  242.2 0.0 all-gather.5.cloned.1.call-start
  242.3 56.1 %all-gather.3.cloned.1.call-done = bf16[1536,1536]{1,0:T(8,128)(2,1)} async-done(((bf16[192,1536]{1,0:T(8,128)(2,1)}), bf16[1536,1536]{1,0:T(8,128)(2,1)}) %all-gather.3.cloned.1.call-update) | async-done | bytes 4718608 | tf_op jit(solution)/shard_map/all_gather | solution.py:26
  298.4 4.4 collective-permute-start.1
  302.8 0.0 copy-start.7
  302.8 0.0 copy-start.2
  302.8 0.0 copy-start.4
  302.8 5.2 fusion.25
  308.0 2.6 collective-permute-start
  310.5 0.0 copy-done.7
  310.6 0.6 dynamic-slice
  311.8 55.5 %collective-permute-done = f32[192,1536]{1,0:T(8,128)} collective-permute-done((f32[192,1536]{1,0:T(8,128)}, f32[192,1536]{1,0:T(8,128)}, u32[]{:S(2)}, u32[]{:S(2)}) %collective-permute-start) | collective-permute-done | bytes 1179680 | tf_op jit(solution)/shard_map/ppermute | solution.py:10
  367.3 0.0 copy-done.2
  367.3 0.0 copy-done.4
  367.3 4.4 fusion.5
  371.8 0.0 copy-start.3
  371.8 0.1 constant_dynamic-slice_fusion.1
  371.9 1.9 gather_fusion
  373.9 0.2 dynamic-update-slice
  374.1 15.5 %all-reduce = bf16[1536]{0:T(1024)(128)(2,1)S(1)} all-reduce(bf16[1536]{0:T(1024)(128)(2,1)S(1)} %dynamic-update-slice), channel_id=1, replica_groups=mesh['tm'=32,'space'=8] {'space'}, use_global_device_ids=true, to_apply=%add | all-reduce | flops 1536 | bytes 6144
  389.6 0.0 collective-permute-done.1
  389.6 0.0 copy-done.3
  389.6 3.4 fusion.7
  393.1 1.9 collective-permute-start.4
  395.0 11.4 %collective-permute-done.4 = bf16[192,1536]{1,0:T(8,128)(2,1)S(1)} collective-permute-done((bf16[192,1536]{1,0:T(8,128)(2,1)S(1)}, bf16[192,1536]{1,0:T(8,128)(2,1)S(1)}, u32[]{:S(2)}, u32[]{:S(2)}) %collective-permute-start.4) | collective-permute-done | bytes 589856 | tf_op jit(solution)/shard_map/ppermute | solution.py:10
  406.4 0.9 broadcast_select_fusion
  407.3 0.0 all-gather.5.cloned.1.call-update
  407.3 57.0 %all-gather.5.cloned.1.call-done = bf16[1536,1536]{1,0:T(8,128)(2,1)} async-done(((bf16[192,1536]{1,0:T(8,128)(2,1)}), bf16[1536,1536]{1,0:T(8,128)(2,1)}) %all-gather.5.cloned.1.call-update) | async-done | bytes 4718608 | tf_op jit(solution)/shard_map/all_gather | solution.py:26
  464.3 4.9 collective-permute-start.5
  469.2 3.9 convolution_convert_fusion.1
  473.2 1.9 collective-permute-start.3
  475.1 5.8 collective-permute-start.2
  480.9 89.7 %collective-permute-done.2 = bf16[1536]{0:T(1024)(128)(2,1)S(1)} collective-permute-done((bf16[1536]{0:T(1024)(128)(2,1)S(1)}, bf16[1536]{0:T(1024)(128)(2,1)S(1)}, u32[]{:S(2)}, u32[]{:S(2)}) %collective-permute-start.2) | collective-permute-done | bytes 3104 | tf_op jit(solution)/shard_map/ppermute | solution.py:10
  570.6 0.0 collective-permute-done.3
  570.6 4.2 fusion.4
  574.8 0.0 copy-start.1
  574.8 0.1 constant_dynamic-slice_fusion
  575.0 1.9 gather_fusion.1
  576.9 0.2 dynamic-update-slice.1
  577.2 15.5 %all-reduce.1 = bf16[1536]{0:T(1024)(128)(2,1)S(1)} all-reduce(bf16[1536]{0:T(1024)(128)(2,1)S(1)} %dynamic-update-slice.1), channel_id=1, replica_groups=mesh['tm'=32,'space'=8] {'space'}, use_global_device_ids=true, to_apply=%add.1 | all-reduce | flops 1536 | bytes 6144
  592.7 0.0 collective-permute-done.5
  592.7 0.0 copy-done.1
  592.7 4.3 fusion.8
  597.0 2.1 collective-permute-start.8
  599.1 3.9 convolution_convert_fusion
  603.0 2.4 collective-permute-start.7
  605.4 5.6 collective-permute-start.6
  611.0 1.3 collective-permute-done.6
  612.3 5.1 collective-permute-done.8
  617.4 0.9 select_bitcast_fusion
  618.3 7.8 %collective-permute-done.7 = bf16[192,1536]{1,0:T(8,128)(2,1)S(1)} collective-permute-done((bf16[192,1536]{1,0:T(8,128)(2,1)S(1)}, bf16[192,1536]{1,0:T(8,128)(2,1)S(1)}, u32[]{:S(2)}, u32[]{:S(2)}) %collective-permute-start.7) | collective-permute-done | bytes 589856 | tf_op jit(solution)/shard_map/ppermute | solution.py:10
  626.1 5.2 fusion.2
  (11 shorter events, 0.1 us)
Async XLA Ops:
  13.1 8.7 %copy-start.6 = (f32[1,1536]{1,0:T(1,128)S(1)}, f32[1,1536]{1,0:T(1,128)}, u32[]{:S(2)}) copy-start(f32[1,1536]{1,0:T(1,128)} %param.7) | copy-start | bytes 18436
  13.1 217.8 %all-to-all-start = ((bf16[8,2,192,1536]{3,2,1,0:T(8,128)(2,1)}), bf16[8,2,192,1536]{3,2,1,0:T(8,128)(2,1)}, u32[]{:S(2)}, u32[]{:S(2)}) async-start(bf16[8,2,192,1536]{3,2,1,0:T(8,128)(2,1)} %stack.5), calls=%async_computation | async-start | bytes 18874368 | tf_op jit(solution)/shard_map/all_to_all | solution.py:65
  21.7 276.7 %all-gather.3.cloned.1.call-start = ((), (), s32[]{:S(2)}) async-start(), calls=%async_computation.1 | async-start | bytes 5308416 | tf_op jit(solution)/shard_map/all_gather | solution.py:26
  230.9 8.8 %copy-start.5 = (bf16[1,192,1536]{2,1,0:T(8,128)(2,1)S(1)}, bf16[1,192,1536]{2,1,0:T(8,128)(2,1)}, u32[]{:S(2)}) copy-start(bf16[1,192,1536]{2,1,0:T(8,128)(2,1)} %param.6) | copy-start | bytes 1769476
  237.4 2.2 copy-start
  242.2 222.1 %all-gather.5.cloned.1.call-start = ((), (), s32[]{:S(2)}) async-start(), calls=%async_computation.2 | async-start | bytes 5308416 | tf_op jit(solution)/shard_map/all_gather | solution.py:26
  298.4 91.2 %collective-permute-start.1 = (bf16[1536,1536]{1,0:T(8,128)(2,1)}, bf16[1536,1536]{1,0:T(8,128)(2,1)}, u32[]{:S(2)}, u32[]{:S(2)}) collective-permute-start(bf16[1536,1536]{1,0:T(8,128)(2,1)} %all-gather.3.cloned.1.call-done), channel_id=1, source_target_pairs={{8,0},{16,8},{24,16},{32,24},{40,32},{48,40},{56,48},{64,56},{72,6... | collective-permute-start | bytes 14155784 | tf_op jit(solution)/shard_map/ppermute | solution.py:10
  302.8 7.8 %copy-start.7 = (u32[256]{0:T(256)S(1)}, u32[256]{0:T(256)}, u32[]{:S(2)}) copy-start(u32[256]{0:T(256)} %constant.83) | copy-start | bytes 3076
  302.8 64.6 %copy-start.2 = (bf16[1,192,1536]{2,1,0:T(8,128)(2,1)S(1)}, bf16[1,192,1536]{2,1,0:T(8,128)(2,1)}, u32[]{:S(2)}) copy-start(bf16[1,192,1536]{2,1,0:T(8,128)(2,1)} %param.5) | copy-start | bytes 1769476
  302.8 64.6 %copy-start.4 = (f32[1,192,1536]{2,1,0:T(8,128)S(1)}, f32[1,192,1536]{2,1,0:T(8,128)}, u32[]{:S(2)}) copy-start(f32[1,192,1536]{2,1,0:T(8,128)} %param.4) | copy-start | bytes 3538948
  308.0 59.4 %collective-permute-start = (f32[192,1536]{1,0:T(8,128)}, f32[192,1536]{1,0:T(8,128)}, u32[]{:S(2)}, u32[]{:S(2)}) collective-permute-start(f32[192,1536]{1,0:T(8,128)} %fusion.25), channel_id=1, source_target_pairs={{8,0},{16,8},{24,16},{32,24},{40,32},{48,40},{56,48},{64,56},{72,6... | collective-permute-start | bytes 3538952 | tf_op jit(solution)/shard_map/ppermute | solution.py:10
  371.8 17.9 %copy-start.3 = (bf16[192,1536]{1,0:T(8,128)(2,1)S(1)}, bf16[192,1536]{1,0:T(8,128)(2,1)}, u32[]{:S(2)}) copy-start(bf16[192,1536]{1,0:T(8,128)(2,1)} %fusion.9) | copy-start | bytes 1769476
  393.1 13.3 %collective-permute-start.4 = (bf16[192,1536]{1,0:T(8,128)(2,1)S(1)}, bf16[192,1536]{1,0:T(8,128)(2,1)S(1)}, u32[]{:S(2)}, u32[]{:S(2)}) collective-permute-start(bf16[192,1536]{1,0:T(8,128)(2,1)S(1)} %fusion.7), channel_id=1, source_target_pairs={{0,8},{8,16},{16,24},{24,32},{32,40},{40,48},{48,56},{56,64},{64,7... | collective-permute-start | bytes 1769480 | tf_op jit(solution)/shard_map/ppermute | solution.py:10
  464.3 128.4 %collective-permute-start.5 = (bf16[1536,1536]{1,0:T(8,128)(2,1)}, bf16[1536,1536]{1,0:T(8,128)(2,1)}, u32[]{:S(2)}, u32[]{:S(2)}) collective-permute-start(bf16[1536,1536]{1,0:T(8,128)(2,1)} %all-gather.5.cloned.1.call-done), channel_id=1, source_target_pairs={{16,0},{24,8},{32,16},{40,24},{48,32},{56,40},{64,48},{72,56},{80,... | collective-permute-start | bytes 14155784 | tf_op jit(solution)/shard_map/ppermute | solution.py:10
  473.2 97.4 %collective-permute-start.3 = (bf16[192,1536]{1,0:T(8,128)(2,1)S(1)}, bf16[192,1536]{1,0:T(8,128)(2,1)S(1)}, u32[]{:S(2)}, u32[]{:S(2)}) collective-permute-start(bf16[192,1536]{1,0:T(8,128)(2,1)S(1)} %convolution_convert_fusion.1), channel_id=1, source_target_pairs={{0,8},{8,16},{16,24},{24,32},{32,40},{40,48},{48,56},{56,64},{64,7... | collective-permute-start | bytes 1769480 | tf_op jit(solution)/shard_map/ppermute | solution.py:10
  475.1 95.5 %collective-permute-start.2 = (bf16[1536]{0:T(1024)(128)(2,1)S(1)}, bf16[1536]{0:T(1024)(128)(2,1)S(1)}, u32[]{:S(2)}, u32[]{:S(2)}) collective-permute-start(bf16[1536]{0:T(1024)(128)(2,1)S(1)} %all-reduce), channel_id=1, source_target_pairs={{8,0},{16,8},{24,16},{32,24},{40,32},{48,40},{56,48},{64,56},{72,6... | collective-permute-start | bytes 9224 | tf_op jit(solution)/shard_map/ppermute | solution.py:10
  574.8 17.9 %copy-start.1 = (bf16[192,1536]{1,0:T(8,128)(2,1)S(1)}, bf16[192,1536]{1,0:T(8,128)(2,1)}, u32[]{:S(2)}) copy-start(bf16[192,1536]{1,0:T(8,128)(2,1)} %broadcast_select_fusion) | copy-start | bytes 1769476
  597.0 20.5 %collective-permute-start.8 = (bf16[192,1536]{1,0:T(8,128)(2,1)}, bf16[192,1536]{1,0:T(8,128)(2,1)S(1)}, u32[]{:S(2)}, u32[]{:S(2)}) collective-permute-start(bf16[192,1536]{1,0:T(8,128)(2,1)} %fusion.8), channel_id=1, source_target_pairs={{0,16},{8,24},{16,32},{24,40},{32,48},{40,56},{48,64},{56,72},{64,... | collective-permute-start | bytes 1769480 | tf_op jit(solution)/shard_map/ppermute | solution.py:10
  603.0 23.1 %collective-permute-start.7 = (bf16[192,1536]{1,0:T(8,128)(2,1)S(1)}, bf16[192,1536]{1,0:T(8,128)(2,1)S(1)}, u32[]{:S(2)}, u32[]{:S(2)}) collective-permute-start(bf16[192,1536]{1,0:T(8,128)(2,1)S(1)} %convolution_convert_fusion), channel_id=1, source_target_pairs={{0,16},{8,24},{16,32},{24,40},{32,48},{40,56},{48,64},{56,72},{64,... | collective-permute-start | bytes 1769480 | tf_op jit(solution)/shard_map/ppermute | solution.py:10
  605.4 6.9 %collective-permute-start.6 = (bf16[1536]{0:T(1024)(128)(2,1)S(1)}, bf16[1536]{0:T(1024)(128)(2,1)S(1)}, u32[]{:S(2)}, u32[]{:S(2)}) collective-permute-start(bf16[1536]{0:T(1024)(128)(2,1)S(1)} %all-reduce.1), channel_id=1, source_target_pairs={{16,0},{24,8},{32,16},{40,24},{48,32},{56,40},{64,48},{72,56},{80,... | collective-permute-start | bytes 9224 | tf_op jit(solution)/shard_map/ppermute | solution.py:10
Sparse Core Ops, SparseCore 0:
  242.3 56.0 all-gather.2
  407.4 56.8 all-gather.4
